TPU v7x, 256 devices: a whole 4x4x8 slice. The times are simulated.
256 devices in a mesh: row: 64 (over z, x, core), rep: 4 (over y).
Axes of the slice: x: 4, y: 4, z: 8, core: 2. Of those that a mesh axis runs over, the one named last changes fastest.
Arguments:
- features: bfloat16 [65536, 128], P('row', 'rep'), may hold values from -6 to 6
- tiles: bfloat16 [512, 16, 128, 128], P('row'), may hold values from -0.1875 to 0.1875
- tile_cols: int32 [512, 16], P('row'), may hold values from 0 to 511, as said below
- counts: int32 [512], P('row'), may hold values from 1 to 16
- weight: bfloat16 [128, 256], P(None, 'rep'), may hold values from -0.5 to 0.5
- bias: float32 [256], P('rep'), may hold values from -3 to 3
- cotangent: bfloat16 [65536, 256], P('row', 'rep'), may hold values from -6 to 6
Outputs:
- hidden: bfloat16 [65536, 256], P('row', 'rep')
- grad_weight: float32 [128, 256], P(None, 'rep')
- grad_bias: float32 [256], P('rep')
- grad_features: bfloat16 [65536, 128], P('row', 'rep')
Inputs may be any that keep to these rules, and one draw needn't show every extreme that they name: `tile_cols`: row block i lies on index i // 8 of row. Every slot of it names a column block lying on an index of row at most two away from that index (cyclically), or on the index half the axis away.
All inputs are finite; a program needn't handle non-finite values.
Results may differ from a plain program's by a relative error of at most 0.007.
Values may be sent and summed in bfloat16 or wider, within the bound.
A program may use at most 128 MiB of HBM per device.

v0:
```python
import jax
import jax.numpy as jnp
from jax import lax
from jax.sharding import PartitionSpec as P


def collect(buffer, shard_rows, tile_cols, live):
    tile_size = buffer.shape[2]
    block_span = shard_rows.shape[0] // tile_size
    shard_blocks = shard_rows.reshape(block_span, tile_size, shard_rows.shape[1])
    wanted = (tile_cols >= 0) & (tile_cols < block_span) & live
    chosen = jnp.take(shard_blocks, jnp.clip(tile_cols, 0, block_span - 1), axis=0)
    return jnp.where(wanted[:, :, None, None], chosen, buffer)


def body(features, tiles, tile_cols, counts, weight, bias, cotangent):
    block_local = tiles.shape[0]
    slot_count = tiles.shape[1]
    tile_size = tiles.shape[2]
    local_rows = features.shape[0]
    width_part = features.shape[1]
    live = jnp.arange(slot_count, dtype=jnp.int32)[None, :] < counts[:, None]
    empty = jnp.zeros((block_local, slot_count, tile_size, width_part), jnp.bfloat16)
    buffer = collect(empty, lax.all_gather(features, "row", axis=0, tiled=True), tile_cols, live)
    agg_part = jnp.einsum("icrk,ickf->irf", tiles, buffer, preferred_element_type=jnp.float32)
    agg_part = agg_part.reshape(local_rows, width_part).astype(jnp.bfloat16)
    agg_whole = lax.all_gather(agg_part, "rep", axis=1, tiled=True)
    pre = jnp.dot(agg_whole, weight, preferred_element_type=jnp.float32) + bias
    hidden = jax.nn.silu(pre).astype(jnp.bfloat16)
    sigma = jax.nn.sigmoid(pre)
    delta = (cotangent.astype(jnp.float32) * sigma * (1.0 + pre * (1.0 - sigma))).astype(
        jnp.bfloat16
    )
    weight_term = lax.dot_general(
        agg_whole, delta, (((0,), (0,)), ((), ())), preferred_element_type=jnp.float32
    )
    bias_term = jnp.sum(delta.astype(jnp.float32), axis=0)
    grad_weight, grad_bias = lax.psum((weight_term, bias_term), "row")
    back_terms = lax.dot_general(
        delta, weight, (((1,), (1,)), ((), ())), preferred_element_type=jnp.float32
    )
    back_agg = lax.psum_scatter(back_terms, "rep", scatter_dimension=1, tiled=True).astype(
        jnp.bfloat16
    )
    back_blocks = back_agg.reshape(block_local, tile_size, width_part)
    contrib = jnp.einsum("icrk,irf->ickf", tiles, back_blocks, preferred_element_type=jnp.float32)
    contrib = contrib.reshape(block_local * slot_count, tile_size, width_part)
    block_span = local_rows * lax.axis_size("row") // tile_size
    wanted = (tile_cols >= 0) & (tile_cols < block_span) & live
    segment_ids = jnp.where(wanted, tile_cols, block_span).reshape(-1)
    summed = jax.ops.segment_sum(contrib, segment_ids, num_segments=block_span + 1)
    grad_features = lax.psum_scatter(
        summed[:block_span].reshape(local_rows * lax.axis_size("row"), width_part),
        "row",
        scatter_dimension=0,
        tiled=True,
    ).astype(jnp.bfloat16)
    return (hidden, grad_weight, grad_bias, grad_features)


def solution(mesh):
    in_specs = (
        P("row", "rep"),
        P("row", None, None, None),
        P("row", None),
        P("row"),
        P(None, "rep"),
        P("rep"),
        P("row", "rep"),
    )
    out_specs = (P("row", "rep"), P(None, "rep"), P("rep"), P("row", "rep"))
    return jax.shard_map(body, mesh=mesh, in_specs=in_specs, out_specs=out_specs, check_vma=False)
```

profile of v0, /device:TPU:1, one launch (start us, length us, event | category | flops | bytes accessed | tf_op | source)
XLA Modules:
  0.0 425.9 jit_solution(13652074373834618355)
XLA Ops:
  7.2 0.0 all-gather.2.cloned.1.call-start
  7.2 0.7 all-gather.2.cloned.1.call-update
  7.9 0.0 reduce-scatter.3.cloned.1.call-start
  8.0 0.8 broadcast_select_fusion
  8.7 0.1 reshape.36
  8.8 0.8 fusion.10
  9.6 84.4 %all-gather.2.cloned.1.call-done = bf16[65536,32]{0,1:T(8,128)(2,1)} async-done(((bf16[1024,32]{0,1:T(8,128)(2,1)}), bf16[65536,32]{0,1:T(8,128)(2,1)}) %all-gather.2.cloned.1.call-update) | async-done | bytes 4194320 | tf_op jit(solution)/shard_map/all_gather | solution.py:24
  94.0 4.9 %copy_bitcast_fusion.1 = bf16[512,128,32]{1,2,0:T(8,128)(2,1)} fusion(bf16[65536,32]{0,1:T(8,128)(2,1)} %all-gather.2.cloned.1.call-done), kind=kLoop, calls=%fused_computation.4 | loop fusion | bytes 8388608 | tf_op jit(solution)/shard_map/reshape | solution.py:10
  98.9 2.9 gather_fusion
  101.9 3.4 fusion.1
  105.3 10.3 %all_gather.7 = bf16[1024,128]{0,1:T(8,128)(2,1)S(1)} all-gather(bf16[1024,32]{0,1:T(8,128)(2,1)S(1)} %bitcast.45), channel_id=1, replica_groups=mesh['row'=64,'rep'=4] {'rep'}, dimensions={1}, use_global_device_ids=true | all-gather | bytes 327680 | tf_op jit(solution)/shard_map/all_gather | solution.py:27
  115.7 1.0 convert_reduce_fusion
  116.7 1.1 fusion.14
  117.8 0.0 reduce-scatter.5.cloned.1.call-start
  117.8 0.1 reshape.44
  117.9 21.2 %reduce-scatter.3.cloned.1.call-done = f32[1024,32]{0,1:T(8,128)} async-done(((f32[1024,128]{0,1:T(8,128)}), f32[1024,32]{0,1:T(8,128)}) %reduce-scatter.3.cloned.1.call-update) | async-done | bytes 131088 | tf_op jit(solution)/shard_map/reduce_scatter | solution.py:42
  139.1 0.9 convert_bitcast_fusion
  140.1 2.9 fusion.8
  142.9 4.3 %broadcast_in_dim.37 = f32[513,128,32]{1,2,0:T(8,128)} broadcast(f32[]{:T(128)} %constant.13.clone.1), dimensions={} | broadcast | bytes 8404996 | tf_op jit(solution)/shard_map/broadcast_in_dim | solution.py:51
  147.2 16.3 %scatter_fusion = f32[513,128,32]{1,2,0:T(8,128)} fusion(f32[513,128,32]{1,2,0:T(8,128)} %broadcast_in_dim.37, s32[128]{0:T(128)S(1)} %reshape.44, f32[128,128,32]{1,2,0:T(8,128)S(1)} %bitcast.42), kind=kCustom, calls=%fused_computation.1 | custom fusion | flops 524288 | bytes 6291968 | tf_op jit(solution)/shard_map/scatter-add | solution.py:51
  163.5 7.1 %copy_bitcast_fusion = f32[65536,32]{0,1:T(8,128)} fusion(f32[513,128,32]{1,2,0:T(8,128)} %scatter_fusion), kind=kLoop, calls=%fused_computation.2 | loop fusion | bytes 16777216 | tf_op jit(solution)/shard_map/reshape | solution.py:53
  170.7 0.2 fusion.13
  170.9 246.9 %all-reduce = (f32[128,64]{0,1:T(8,128)}, f32[64]{0:T(128)}) all-reduce(f32[128,64]{0,1:T(8,128)S(1)} %fusion.13, f32[64]{0:T(128)S(1)} %get-tuple-element.6), channel_id=1, replica_groups=mesh['row'=64,'rep'=4] {'row'}, use_global_device_ids=true, to_apply=%region_0.1 | all-reduce | flops 8256 | bytes 66048 | tf_op jit(solution)/shard_map/psum | solution.py:38
  417.8 1.5 convert_element_type.35
  (12 shorter events, 0.1 us)
Async XLA Ops:
  7.2 108.5 %copy-start = (bf16[128,64]{0,1:T(8,128)(2,1)S(1)}, bf16[128,64]{0,1:T(8,128)(2,1)}, u32[]{:S(2)}) copy-start(bf16[128,64]{0,1:T(8,128)(2,1)} %param.11) | copy-start | bytes 49156
  7.2 86.8 %all-gather.2.cloned.1.call-start = ((), (), s32[]{:S(2)}) async-start(), calls=%async_computation.2 | async-start | bytes 4259840 | tf_op jit(solution)/shard_map/all_gather | solution.py:24
  7.9 131.2 %reduce-scatter.3.cloned.1.call-start = ((), (), s32[]{:S(2)}) async-start(), calls=%async_computation.3 | async-start | bytes 655360 | tf_op jit(solution)/shard_map/reduce_scatter | solution.py:42
  101.8 13.8 %copy-start.1 = (bf16[1024,64]{0,1:T(8,128)(2,1)S(1)}, bf16[1024,64]{0,1:T(8,128)(2,1)}, u32[]{:S(2)}) copy-start(bf16[1024,64]{0,1:T(8,128)(2,1)} %param.13) | copy-start | bytes 393220
  101.8 13.8 %copy-start.2 = (f32[64]{0:T(128)S(1)}, f32[64]{0:T(128)}, u32[]{:S(2)}) copy-start(f32[64]{0:T(128)} %param.12) | copy-start | bytes 772
  117.8 300.0 %reduce-scatter.5.cloned.1.call-start = ((), (), s32[]{:S(2)}) async-start(), calls=%async_computation.4 | async-start | bytes 8519680 | tf_op jit(solution)/shard_map/reduce_scatter | solution.py:52
Sparse Core Ops, SparseCore 0:
  10.8 83.1 all-gather.1
  117.9 21.1 reduce-scatter.2
  170.8 148.7 reduce-scatter.4
where the time goes:
time: 430 us; the launch traced here: 426 us
  blocking collectives  257 us (60%)
  waiting for transfers between devices  106 us (25%)
  other arithmetic  20.3 us (5%)
  local copies, waits for them, and re-layouts  19.5 us (5%)
  between operations  13.8 us (3%)
  matrix products  8.58 us (2%)
    psum x1, blocking collectives, body(): grad_weight, grad_bias = lax.psum((weight_term, bias_term), 'row')  247 us
    all_gather x1, waiting for transfers between devices, body(): lax.all_gather(features, 'row', axis=0, tiled=True)  84.4 us
    reduce_scatter x1, waiting for transfers between devices, body(): lax.psum_scatter(back_terms, 'rep', scatter_dimension=1, tiled=True)  21.2 us
    scatter-add x1, other arithmetic, body(): jax.ops.segment_sum(contrib, segment_ids, num_segments=block_span + 1)  16.3 us
    all_gather x1, blocking collectives, body(): agg_whole = lax.all_gather(agg_part, 'rep', axis=1, tiled=True)  10.3 us
  transfers between devices with their start and end apart: 3, of which 2 were waited for; matrix products, arithmetic and copies ran while one was open for 0% of the time, Pallas kernels for 0%

commit v1 on v0

v1 whole, which is shorter than its diff:
```python
import functools

import jax
import jax.numpy as jnp
from jax import lax
from jax.experimental import pallas as pl
from jax.experimental.pallas import tpu as pltpu
from jax.sharding import PartitionSpec as P

F32 = jnp.float32
BF16 = jnp.bfloat16
TILE = 128
OFFSETS = (-2, -1, 0, 1, 2, None)
OWN = 2
NT = (((1,), (1,)), ((), ()))
NN = (((1,), (0,)), ((), ()))


def dot(a, b, dims):
    return lax.dot_general(a, b, dims, preferred_element_type=F32)


def kernel(
    n_row, n_rep, plane,
    cols_ref, counts_ref, bias_ref, ft_ref, tiles_ref, wt_ref, ct_ref,
    hid_out, gw_out, gb_out, gf_out,
    tiles, feats, cots, weights, biases, weight_fh, bias_col, keys_2d, table, table_s,
    agg_mine, agg, hid_mine, delta, back_mine, back, run, part, part_in,
    s1_mine, s1_in, s2_mine, s2_in, s3_mine, s3_in, gw_mine,
    sem_feat, sem_tile, sem_local,
    ss_feat, rs_feat, ss_pre, rs_pre, ss_agg, rs_agg, ss_back, rs_back, ss_hid, rs_hid,
    ss_s1, rs_s1, ss_s2, rs_s2, ss_s3, rs_s3, ss_s4, rs_s4, ss_part, rs_part,
):
    row = lax.axis_index("row")
    rep = lax.axis_index("rep")
    depth = n_row // plane
    layer = row // plane
    spot = row % plane
    n_blk = tiles_ref.shape[0]
    n_slot = tiles_ref.shape[1]
    per = n_blk // n_rep
    span = per * TILE
    none_feat = len(OFFSETS) * n_blk
    n_slots = n_blk * n_slot
    offsets = [n_row // 2 if o is None else o for o in OFFSETS]
    far_first = (5, 0, 4, 1, 3)
    order = tuple(range(1, n_rep)) + (0,)

    def block_at(p):
        return (per * rep + p) % n_blk

    def row_at(offset):
        return {"row": (row + offset + n_row) % n_row, "rep": rep}

    def rep_at(k):
        return {"row": row, "rep": (rep + k) % n_rep}

    def spot_at(k):
        return {"row": layer * plane + (spot + k) % plane, "rep": rep}

    def layer_at(k):
        return {"row": ((layer + k) % depth) * plane + spot, "rep": rep}

    def send(src, dst, ss, rs, where):
        return pltpu.make_async_remote_copy(
            src_ref=src, dst_ref=dst, send_sem=ss, recv_sem=rs,
            device_id=where, device_id_type=pl.DeviceIdType.MESH,
        )

    feat_loads = [
        pltpu.make_async_copy(ft_ref.at[:, TILE * b:TILE * (b + 1)], feats.at[OWN * n_blk + b], sem_feat.at[b])
        for b in range(n_blk)
    ]
    for c in feat_loads:
        c.start()
    mine = pl.ds(pl.multiple_of(rep * span, span), span)
    load_w = pltpu.make_async_copy(wt_ref, weights.at[rep], sem_local.at[0])
    load_c = pltpu.make_async_copy(ct_ref.at[:, mine], cots.at[rep], sem_local.at[1])
    load_w.start()
    load_c.start()
    tile_loads = []
    for k in range(n_rep):
        which = pl.ds(((rep + k) % n_rep) * per, per)
        tile_loads.append(
            pltpu.make_async_copy(tiles_ref.at[which], tiles.at[which], sem_tile.at[k])
        )
    for k in order:
        tile_loads[k].start()

    barrier = pltpu.get_barrier_semaphore()
    peers = [row_at(offsets[g]) for g in far_first]
    peers += [rep_at(k) for k in range(1, n_rep)]
    peers += [spot_at(k) for k in range(1, plane)]
    peers += [layer_at(k) for k in range(1, depth)]
    for where in peers:
        pl.semaphore_signal(barrier, inc=1, device_id=where, device_id_type=pl.DeviceIdType.MESH)
    biases[rep] = jnp.broadcast_to(jnp.pad(bias_ref[...], ((0, 0), (0, TILE - bias_ref.shape[1]))), (8, TILE))
    pl.semaphore_wait(barrier, len(peers))

    for c in feat_loads:
        c.wait()
    feat_sends = {
        g: send(
            feats.at[OWN * n_blk:(OWN + 1) * n_blk], feats.at[g * n_blk:(g + 1) * n_blk],
            ss_feat.at[g], rs_feat.at[g], row_at(-offsets[g]),
        )
        for g in far_first
    }
    for g in far_first:
        feat_sends[g].start()
    load_w.wait()
    pre_sends = []
    for k in range(1, n_rep):
        pre_sends.append(send(weights.at[rep], weights.at[rep], ss_pre.at[0, k - 1], rs_pre.at[0, k - 1], rep_at(k)))
        pre_sends.append(send(biases.at[rep], biases.at[rep], ss_pre.at[1, k - 1], rs_pre.at[1, k - 1], rep_at(k)))
        pre_sends.append(
            send(
                ct_ref.at[:, pl.ds(pl.multiple_of(((rep + k) % n_rep) * span, span), span)],
                cots.at[rep], ss_pre.at[2, k - 1], rs_pre.at[2, k - 1], rep_at(k),
            )
        )
    for c in pre_sends:
        c.start()

    cols = cols_ref[...]
    shape = cols.shape
    slot = lax.broadcasted_iota(jnp.int32, shape, 1)
    line = lax.broadcasted_iota(jnp.int32, shape, 0)
    count = jnp.zeros(shape, jnp.int32)
    for i in range(n_blk):
        count = jnp.where(line == i, counts_ref[i], count)
    group = jnp.minimum((cols // n_blk - row + 2 + n_row) % n_row, 5)
    key = jnp.where(slot < count, group * n_blk + cols % n_blk, none_feat)
    keys_2d[:, 0:n_slot] = key
    keys = jnp.concatenate([keys_2d[pl.ds(block_at(p), 1), 0:n_slot] for p in range(n_blk)], axis=1)
    by_lane = jnp.broadcast_to(keys, (n_slots, n_slots))
    by_line = by_lane.T
    up = lax.broadcasted_iota(jnp.int32, (n_slots, n_slots), 0)
    across = lax.broadcasted_iota(jnp.int32, (n_slots, n_slots), 1)
    before = jnp.max(jnp.where((by_line == by_lane) & (up < across), up, -1), axis=0, keepdims=True)
    last = jnp.max(jnp.where(by_line == across, up, -1), axis=0, keepdims=True)
    table[0:1, :] = keys
    table[1:2, :] = jnp.where(before < 0, n_slots, before)
    table[2:3, :] = jnp.where(last < 0, n_slots, last)
    table[3:8, :] = jnp.zeros((5, n_slots), jnp.int32)
    to_scalar = pltpu.make_async_copy(table, table_s, sem_local.at[2])
    to_scalar.start()
    feats[none_feat] = jnp.zeros(feats.shape[1:], BF16)
    run[n_slots] = jnp.zeros(run.shape[1:], F32)
    to_scalar.wait()

    for c in pre_sends:
        c.wait_recv()
    load_c.wait()
    n_hid = weights.shape[1]
    for j in range(n_rep):
        weight_fh[:, j * n_hid:(j + 1) * n_hid] = weights[j].astype(F32).T.astype(BF16)
        bias_col[j] = jnp.broadcast_to(biases[j, 0:1, :], (TILE, TILE)).T[0:n_hid, :]

    for g in far_first:
        feat_sends[g].wait_recv()

    agg_sends = []
    for k in order:
        tile_loads[k].wait()
        for q in range(per):
            p = k * per + q
            i = block_at(p)
            total = jnp.zeros((feats.shape[1], TILE), F32)
            for s in range(n_slot):
                total += dot(feats[table_s[0, p * n_slot + s]], tiles[i, s], NT)
            agg_mine[k, :, q * TILE:(q + 1) * TILE] = total.astype(BF16)
        if k:
            c = send(agg_mine.at[k], agg.at[rep], ss_agg.at[k - 1], rs_agg.at[k - 1], rep_at(k))
            c.start()
            agg_sends.append(c)
    agg[rep] = agg_mine[0]
    for c in agg_sends:
        c.wait_recv()

    whole = agg[...].reshape(n_rep * agg.shape[1], span)
    hid_sends = []
    for j in range(n_rep):
        wide_bias = jnp.concatenate([bias_col[j]] * (span // TILE), axis=1)
        pre = dot(weights[j], whole, NN) + wide_bias
        sigma = jax.nn.sigmoid(pre)
        hid_mine[j] = (pre * sigma).astype(BF16)
        delta[j] = (cots[j].astype(F32) * sigma * (1.0 + pre * (1.0 - sigma))).astype(BF16)
    deltas = delta[...].reshape(n_rep * n_hid, span)
    back_full = dot(weight_fh[...], deltas, NN).astype(BF16)
    back_mine[...] = back_full.reshape(back_mine.shape)
    back_sends = []
    for k in range(1, n_rep):
        c = send(back_mine.at[(rep + k) % n_rep], back.at[rep], ss_back.at[k - 1], rs_back.at[k - 1], rep_at(k))
        c.start()
        back_sends.append(c)
    back[rep] = back_mine[rep]
    for k in range(1, n_rep):
        c = send(hid_mine.at[(rep + k) % n_rep], hid_out.at[:, mine], ss_hid.at[k - 1], rs_hid.at[k - 1], rep_at(k))
        c.start()
        hid_sends.append(c)
    keep_hid = pltpu.make_async_copy(hid_mine.at[rep], hid_out.at[:, mine], sem_local.at[3])
    keep_hid.start()
    ones = jnp.ones((8, span), BF16)
    for j in range(n_rep):
        s1_mine[j, 0:n_hid, :] = dot(delta[j], whole, NT)
        s1_mine[j, n_hid:n_hid + 8, :] = jnp.pad(dot(ones, delta[j], NT), ((0, 0), (0, TILE - n_hid)))
    s1_sends = []
    for k in range(1, n_rep):
        c = send(s1_mine.at[(rep + k) % n_rep], s1_in.at[k - 1], ss_s1.at[k - 1], rs_s1.at[k - 1], rep_at(k))
        c.start()
        s1_sends.append(c)

    for c in back_sends:
        c.wait_recv()

    for k in range(n_rep):
        chunk = (rep + k) % n_rep
        for q in range(per):
            p = k * per + q
            i = block_at(p)
            lhs = back[chunk, :, q * TILE:(q + 1) * TILE]
            for s in range(n_slot):
                t = p * n_slot + s
                run[t] = dot(lhs, tiles[i, s], NN) + run[table_s[1, t]]

    part_sends = {}
    for g in far_first:
        for b in range(n_blk):
            part[g, b] = run[table_s[2, g * n_blk + b]].astype(BF16)
        c = send(part.at[g], part_in.at[g], ss_part.at[g], rs_part.at[g], row_at(offsets[g]))
        c.start()
        part_sends[g] = c

    for c in s1_sends:
        c.wait_recv()
    mid = s1_mine[rep]
    for k in range(1, n_rep):
        mid += s1_in[k - 1]
    for m in range(plane):
        s2_mine[m, 0:8, :] = mid[8 * m:8 * (m + 1), :]
        s2_mine[m, 8:16, :] = mid[n_hid:n_hid + 8, :]
    s2_sends = []
    for k in range(1, plane):
        c = send(s2_mine.at[(spot + k) % plane], s2_in.at[spot], ss_s2.at[k - 1], rs_s2.at[k - 1], spot_at(k))
        c.start()
        s2_sends.append(c)
    s2_in[spot] = s2_mine[spot]
    for c in s2_sends:
        c.wait_recv()
    s3_mine[...] = sum(s2_in[m] for m in range(plane))
    s3_sends = []
    for k in range(1, depth):
        c = send(s3_mine, s3_in.at[layer], ss_s3.at[k - 1], rs_s3.at[k - 1], layer_at(k))
        c.start()
        s3_sends.append(c)
    s3_in[layer] = s3_mine[...]
    for c in s3_sends:
        c.wait_recv()
    done = sum(s3_in[m] for m in range(depth))
    gw_mine[...] = done[0:8, :]
    gb_out[...] = done[8:16, :]
    my_rows = pl.ds(pl.multiple_of(spot * 8, 8), 8)
    s4_sends = []
    for k in range(1, plane):
        c = send(gw_mine, gw_out.at[my_rows, :], ss_s4.at[k - 1], rs_s4.at[k - 1], spot_at(k))
        c.start()
        s4_sends.append(c)
    keep_gw = pltpu.make_async_copy(gw_mine, gw_out.at[my_rows, :], sem_local.at[4])
    keep_gw.start()

    for g in far_first:
        part_sends[g].wait_recv()
    for b in range(n_blk):
        value = run[table_s[2, OWN * n_blk + b]]
        for g in far_first:
            value += part_in[g, b].astype(F32)
        gf_out[:, b * TILE:(b + 1) * TILE] = value.astype(BF16)

    for c in hid_sends + s4_sends:
        c.wait_recv()
    keep_hid.wait()
    keep_gw.wait()
    everything = [feat_sends[g] for g in far_first] + pre_sends + agg_sends + back_sends + hid_sends
    everything += s1_sends + s2_sends + s3_sends + s4_sends + [part_sends[g] for g in far_first]
    for c in everything:
        c.wait_send()


def body(n_row, n_rep, plane, features, tiles, tile_cols, counts, weight, bias, cotangent):
    n_blk, n_slot = tiles.shape[:2]
    rows, width = features.shape
    n_hid = weight.shape[1]
    fin = weight.shape[0]
    span = rows // n_rep
    depth = n_row // plane
    n_far = len(OFFSETS)
    n_slots = n_blk * n_slot
    dma = pltpu.SemaphoreType.DMA
    vmem = pl.BlockSpec(memory_space=pltpu.VMEM)
    smem = pl.BlockSpec(memory_space=pltpu.SMEM)
    hbm = pl.BlockSpec(memory_space=pl.ANY)

    def pair(*shape):
        return [dma(shape), dma(shape)]

    out = pl.pallas_call(
        functools.partial(kernel, n_row, n_rep, plane),
        out_shape=(
            jax.ShapeDtypeStruct((n_hid, rows), BF16),
            jax.ShapeDtypeStruct((n_hid, fin), F32),
            jax.ShapeDtypeStruct((8, TILE), F32),
            jax.ShapeDtypeStruct((width, rows), BF16),
        ),
        in_specs=[vmem, smem, vmem, hbm, hbm, hbm, hbm],
        out_specs=(vmem, vmem, vmem, vmem),
        scratch_shapes=[
            pltpu.VMEM(tiles.shape, BF16),
            pltpu.VMEM((len(OFFSETS) * n_blk + 1, width, TILE), BF16),
            pltpu.VMEM((n_rep, n_hid, span), BF16),
            pltpu.VMEM((n_rep, n_hid, fin), BF16),
            pltpu.VMEM((n_rep, 8, TILE), F32),
            pltpu.VMEM((fin, n_rep * n_hid), BF16),
            pltpu.VMEM((n_rep, n_hid, TILE), F32),
            pltpu.VMEM((n_blk, TILE), jnp.int32),
            pltpu.VMEM((8, TILE), jnp.int32),
            pltpu.SMEM((8, TILE), jnp.int32),
            pltpu.VMEM((n_rep, width, span), BF16),
            pltpu.VMEM((n_rep, width, span), BF16),
            pltpu.VMEM((n_rep, n_hid, span), BF16),
            pltpu.VMEM((n_rep, n_hid, span), BF16),
            pltpu.VMEM((n_rep, width, span), BF16),
            pltpu.VMEM((n_rep, width, span), BF16),
            pltpu.VMEM((n_slots + 1, width, TILE), F32),
            pltpu.VMEM((n_far, n_blk, width, TILE), BF16),
            pltpu.VMEM((n_far, n_blk, width, TILE), BF16),
            pltpu.VMEM((n_rep, n_hid + 8, TILE), F32),
            pltpu.VMEM((n_rep - 1, n_hid + 8, TILE), F32),
            pltpu.VMEM((plane, 16, TILE), F32),
            pltpu.VMEM((plane, 16, TILE), F32),
            pltpu.VMEM((16, TILE), F32),
            pltpu.VMEM((depth, 16, TILE), F32),
            pltpu.VMEM((8, TILE), F32),
            dma((n_blk,)),
            dma((n_rep,)),
            dma((5,)),
            *pair(n_far),
            *pair(3, n_rep - 1),
            *pair(n_rep - 1),
            *pair(n_rep - 1),
            *pair(n_rep - 1),
            *pair(n_rep - 1),
            *pair(plane - 1),
            *pair(depth - 1),
            *pair(plane - 1),
            *pair(n_far),
        ],
        compiler_params=pltpu.CompilerParams(
            collective_id=0, has_side_effects=True, vmem_limit_bytes=32 * 1024 * 1024
        ),
        cost_estimate=pl.CostEstimate(
            flops=4 * n_slots * TILE * TILE * width, bytes_accessed=tiles.size * 2, transcendentals=span * n_rep * n_hid
        ),
    )(
        tile_cols, counts, bias.reshape(1, n_hid), features.T, tiles, weight.T, cotangent.T,
    )
    hidden, grad_weight, grad_bias, grad_features = out
    return hidden.T, grad_weight.T, grad_bias[0, :n_hid], grad_features.T


def solution(mesh):
    in_specs = (
        P("row", "rep"),
        P("row", None, None, None),
        P("row", None),
        P("row"),
        P(None, "rep"),
        P("rep"),
        P("row", "rep"),
    )
    out_specs = (P("row", "rep"), P(None, "rep"), P("rep"), P("row", "rep"))
    n_row, n_rep = mesh.shape["row"], mesh.shape["rep"]
    step = functools.partial(body, n_row, n_rep, 8)
    return jax.shard_map(step, mesh=mesh, in_specs=in_specs, out_specs=out_specs, check_vma=False)
```

time: 430 us -> 54.7 us (0.13)
  blocking collectives: 257 us -> 0 us
  waiting for transfers between devices: 106 us -> 0 us
  Pallas kernels: 0 us -> 44.7 us
  other arithmetic: 20.3 us -> 0 us
  between operations: 13.8 us -> 0.66 us
  local copies, waits for them, and re-layouts: 19.5 us -> 9.05 us
  matrix products: 8.58 us -> 0 us
    psum x1 -> x0, blocking collectives: 247 us -> none  [body(): grad_weight, grad_bias = lax.psum((weight_term, bias_term), 'row')]
    all_gather x1 -> x0, waiting for transfers between devices: 84.4 us -> none  [body(): lax.all_gather(features, 'row', axis=0, tiled=True)]
    pallas_call x0 -> x1, Pallas kernels: none -> 44.7 us  [body(): pl.pallas_call(functools.partial(kernel, n_row, n_rep, plane), out_shape=...]
    reduce_scatter x2 -> x0, waiting for transfers between devices: 21.2 us -> none  [the longest x1 21.2 us: body(): lax.psum_scatter(back_terms, 'rep', scatter_dimension=1, tiled=True)]
    scatter-add x1 -> x0, other arithmetic: 16.3 us -> none  [body(): jax.ops.segment_sum(contrib, segment_ids, num_segments=block_span + 1)]
    reshape x2 -> x0, local copies, waits for them, and re-layouts: 12 us -> none  [the longest x1 7.15 us: body(): summed[:block_span].reshape(local_rows * lax.axis_size('row'), width_part)]
    all_gather x1 -> x0, blocking collectives: 10.3 us -> none  [body(): agg_whole = lax.all_gather(agg_part, 'rep', axis=1, tiled=True)]
    dot_general x5 -> x0, matrix products: 8.58 us -> none  [the longest x1 3.41 us: body(): jnp.einsum('icrk,ickf->irf', tiles, buffer, preferred_element_type=jnp.fl...]
  transfers between devices with their start and end apart: 3 -> 0, of which waited for: 2 -> 0; matrix products, arithmetic and copies ran while one was open for 0% -> 0% of each run, Pallas kernels for 0% -> 0%
where the time goes in v1:
time: 54.7 us; the launch traced here: 54.4 us
  Pallas kernels  44.7 us (82%)
  local copies, waits for them, and re-layouts  9.05 us (17%)
  between operations  0.66 us (1%)
    pallas_call x1, Pallas kernels, body(): pl.pallas_call(functools.partial(kernel, n_row, n_rep, plane), out_shape=...  44.7 us
    unnamed x17, local copies, waits for them, and re-layouts  8.53 us

profile of v1, /device:TPU:1, one launch (start us, length us, event | category | flops | bytes accessed | tf_op | source)
XLA Modules:
  0.0 54.4 jit_solution(4676318715441158922)
XLA Ops:
  0.6 0.0 copy-start
  0.6 2.2 %copy-done = bf16[8,16,128,128]{3,2,1,0:T(8,128)(2,1)S(1)} copy-done((bf16[8,16,128,128]{3,2,1,0:T(8,128)(2,1)S(1)}, bf16[8,16,128,128]{3,2,1,0:T(8,128)(2,1)}, u32[]{:S(2)}) %copy-start) | copy-done | bytes 4194328
  2.8 0.0 copy-start.1
  2.8 0.9 %copy-done.1 = bf16[1024,64]{0,1:T(8,128)(2,1)S(1)} copy-done((bf16[1024,64]{0,1:T(8,128)(2,1)S(1)}, bf16[1024,64]{0,1:T(8,128)(2,1)}, u32[]{:S(2)}) %copy-start.1) | copy-done | bytes 131096
  3.7 0.0 copy-start.2
  3.7 0.8 %copy-done.2 = bf16[1024,32]{0,1:T(8,128)(2,1)S(1)} copy-done((bf16[1024,32]{0,1:T(8,128)(2,1)S(1)}, bf16[1024,32]{0,1:T(8,128)(2,1)}, u32[]{:S(2)}) %copy-start.2) | copy-done | bytes 65560
  4.6 0.0 copy-start.3
  4.6 0.7 %copy-done.3 = bf16[128,64]{0,1:T(8,128)(2,1)S(1)} copy-done((bf16[128,64]{0,1:T(8,128)(2,1)S(1)}, bf16[128,64]{0,1:T(8,128)(2,1)}, u32[]{:S(2)}) %copy-start.3) | copy-done | bytes 16408
  5.3 0.0 copy-start.4
  5.3 0.7 %copy-done.4 = s32[8,16]{1,0:T(8,128)S(1)} copy-done((s32[8,16]{1,0:T(8,128)S(1)}, s32[8,16]{1,0:T(8,128)}, u32[]{:S(2)}) %copy-start.4) | copy-done | bytes 536
  6.0 0.0 copy-start.5
  6.0 0.7 %copy-done.5 = s32[8]{0:T(128)S(1)} copy-done((s32[8]{0:T(128)S(1)}, s32[8]{0:T(128)}, u32[]{:S(2)}) %copy-start.5) | copy-done | bytes 56
  6.6 0.0 copy-start.6
  6.6 0.7 %copy-done.6 = f32[64]{0:T(128)S(1)} copy-done((f32[64]{0:T(128)S(1)}, f32[64]{0:T(128)}, u32[]{:S(2)}) %copy-start.6) | copy-done | bytes 280
  7.3 44.7 %shard_map.102 = (bf16[64,1024]{1,0:T(8,128)(2,1)S(1)}, f32[64,128]{1,0:T(8,128)S(1)}, f32[8,128]{1,0:T(8,128)S(1)}, bf16[32,1024]{1,0:T(8,128)(2,1)S(1)}) custom-call(s32[8,16]{1,0:T(8,128)S(1)} %copy-done.4, s32[8]{0:T(128)S(1)} %copy-done.5, f32[1,64]{1,0:T(1,128)S(1)} %bitcast.15, bf16[32,1024]{1,0:T(8,128)(2,1)S(1)} %bitcast.11, ...), custom_call_target="tpu_custom_call" | custom-call | flops 268435456 | bytes 4194304 | tf_op jit(solution)/shard_map/pallas_call | solution.py:307
  52.0 0.5 slice_bitcast_fusion
  52.5 0.7 %copy.14 = bf16[1024,64]{0,1:T(8,128)(2,1)} copy(bf16[1024,64]{0,1:T(8,128)(2,1)S(1)} %bitcast.10) | data formatting | bytes 262144
  53.2 0.6 %copy.15 = f32[128,64]{0,1:T(8,128)} copy(f32[128,64]{0,1:T(8,128)S(1)} %bitcast.13) | data formatting | bytes 65536
  53.8 0.6 %copy.16 = bf16[1024,32]{0,1:T(8,128)(2,1)} copy(bf16[1024,32]{0,1:T(8,128)(2,1)S(1)} %bitcast.12) | data formatting | bytes 131072
Async XLA Ops:
  0.6 2.2 %copy-start = (bf16[8,16,128,128]{3,2,1,0:T(8,128)(2,1)S(1)}, bf16[8,16,128,128]{3,2,1,0:T(8,128)(2,1)}, u32[]{:S(2)}) copy-start(bf16[8,16,128,128]{3,2,1,0:T(8,128)(2,1)} %tiles_ref.1) | copy-start | bytes 12582916
  2.8 0.9 %copy-start.1 = (bf16[1024,64]{0,1:T(8,128)(2,1)S(1)}, bf16[1024,64]{0,1:T(8,128)(2,1)}, u32[]{:S(2)}) copy-start(bf16[1024,64]{0,1:T(8,128)(2,1)} %param.13) | copy-start | bytes 393220
  3.7 0.8 %copy-start.2 = (bf16[1024,32]{0,1:T(8,128)(2,1)S(1)}, bf16[1024,32]{0,1:T(8,128)(2,1)}, u32[]{:S(2)}) copy-start(bf16[1024,32]{0,1:T(8,128)(2,1)} %param.7) | copy-start | bytes 196612
  4.6 0.7 %copy-start.3 = (bf16[128,64]{0,1:T(8,128)(2,1)S(1)}, bf16[128,64]{0,1:T(8,128)(2,1)}, u32[]{:S(2)}) copy-start(bf16[128,64]{0,1:T(8,128)(2,1)} %param.11) | copy-start | bytes 49156
  5.3 0.7 %copy-start.4 = (s32[8,16]{1,0:T(8,128)S(1)}, s32[8,16]{1,0:T(8,128)}, u32[]{:S(2)}) copy-start(s32[8,16]{1,0:T(8,128)} %cols_ref.1) | copy-start | bytes 1540
  6.0 0.7 %copy-start.5 = (s32[8]{0:T(128)S(1)}, s32[8]{0:T(128)}, u32[]{:S(2)}) copy-start(s32[8]{0:T(128)} %counts_ref.1) | copy-start | bytes 100
  6.6 0.7 %copy-start.6 = (f32[64]{0:T(128)S(1)}, f32[64]{0:T(128)}, u32[]{:S(2)}) copy-start(f32[64]{0:T(128)} %param.12) | copy-start | bytes 772

commit v2 on v1

--- a/solution.py
+++ b/solution.py
@@ -22,14 +22,14 @@
 
 def kernel(
     n_row, n_rep, plane,
-    cols_ref, counts_ref, bias_ref, ft_ref, tiles_ref, wt_ref, ct_ref,
+    cols_hbm, counts_hbm, bias_hbm, ft_ref, tiles_ref, wt_ref, ct_ref,
     hid_out, gw_out, gb_out, gf_out,
-    tiles, feats, cots, weights, biases, weight_fh, bias_col, keys_2d, table, table_s,
+    cols_ref, counts_ref, bias_ref, tiles, feats, cots, weights, biases, weight_fh, bias_col, keys_2d, table, table_s,
     agg_mine, agg, hid_mine, delta, back_mine, back, run, part, part_in,
-    s1_mine, s1_in, s2_mine, s2_in, s3_mine, s3_in, gw_mine,
+    team_mine, team_in, s3_mine, s3_in, gw_mine, gb_mine, gf_mine,
     sem_feat, sem_tile, sem_local,
     ss_feat, rs_feat, ss_pre, rs_pre, ss_agg, rs_agg, ss_back, rs_back, ss_hid, rs_hid,
-    ss_s1, rs_s1, ss_s2, rs_s2, ss_s3, rs_s3, ss_s4, rs_s4, ss_part, rs_part,
+    ss_team, rs_team, ss_s3, rs_s3, ss_s4, rs_s4, ss_part, rs_part,
 ):
     row = lax.axis_index("row")
     rep = lax.axis_index("rep")
@@ -44,16 +44,23 @@
     n_slots = n_blk * n_slot
     offsets = [n_row // 2 if o is None else o for o in OFFSETS]
     far_first = (5, 0, 4, 1, 3)
-    order = tuple(range(1, n_rep)) + (0,)
-
-    def block_at(p):
-        return (per * rep + p) % n_blk
+    hops = [min(k, n_rep - k) for k in range(n_rep)]
+    near_last = sorted(range(1, n_rep), key=lambda k: -hops[k])
+    order = near_last + [0]
+    team = [(k, m) for k in range(n_rep) for m in range(plane) if (k, m) != (0, 0)]
+    back_order = [0] + near_last[::-1]
+
+    def block_at(p, q=0):
+        return ((rep + back_order[p // per]) % n_rep) * per + p % per + q
 
     def row_at(offset):
         return {"row": (row + offset + n_row) % n_row, "rep": rep}
 
     def rep_at(k):
         return {"row": row, "rep": (rep + k) % n_rep}
+
+    def team_at(k, m):
+        return {"row": layer * plane + (spot + m) % plane, "rep": (rep + k) % n_rep}
 
     def spot_at(k):
         return {"row": layer * plane + (spot + k) % plane, "rep": rep}
@@ -67,6 +74,13 @@
             device_id=where, device_id_type=pl.DeviceIdType.MESH,
         )
 
+    barrier = pltpu.get_barrier_semaphore()
+    peers = [row_at(offsets[g]) for g in far_first]
+    peers += [team_at(*o) for o in team]
+    peers += [layer_at(k) for k in range(1, depth)]
+    for where in peers:
+        pl.semaphore_signal(barrier, inc=1, device_id=where, device_id_type=pl.DeviceIdType.MESH)
+
     feat_loads = [
         pltpu.make_async_copy(ft_ref.at[:, TILE * b:TILE * (b + 1)], feats.at[OWN * n_blk + b], sem_feat.at[b])
         for b in range(n_blk)
@@ -76,8 +90,11 @@
     mine = pl.ds(pl.multiple_of(rep * span, span), span)
     load_w = pltpu.make_async_copy(wt_ref, weights.at[rep], sem_local.at[0])
     load_c = pltpu.make_async_copy(ct_ref.at[:, mine], cots.at[rep], sem_local.at[1])
-    load_w.start()
-    load_c.start()
+    load_cols = pltpu.make_async_copy(cols_hbm, cols_ref, sem_local.at[5])
+    load_counts = pltpu.make_async_copy(counts_hbm, counts_ref, sem_local.at[6])
+    load_bias = pltpu.make_async_copy(bias_hbm, bias_ref, sem_local.at[7])
+    for c in (load_w, load_bias, load_cols, load_counts, load_c):
+        c.start()
     tile_loads = []
     for k in range(n_rep):
         which = pl.ds(((rep + k) % n_rep) * per, per)
@@ -87,14 +104,6 @@
     for k in order:
         tile_loads[k].start()
 
-    barrier = pltpu.get_barrier_semaphore()
-    peers = [row_at(offsets[g]) for g in far_first]
-    peers += [rep_at(k) for k in range(1, n_rep)]
-    peers += [spot_at(k) for k in range(1, plane)]
-    peers += [layer_at(k) for k in range(1, depth)]
-    for where in peers:
-        pl.semaphore_signal(barrier, inc=1, device_id=where, device_id_type=pl.DeviceIdType.MESH)
-    biases[rep] = jnp.broadcast_to(jnp.pad(bias_ref[...], ((0, 0), (0, TILE - bias_ref.shape[1]))), (8, TILE))
     pl.semaphore_wait(barrier, len(peers))
 
     for c in feat_loads:
@@ -109,6 +118,8 @@
     for g in far_first:
         feat_sends[g].start()
     load_w.wait()
+    load_bias.wait()
+    biases[rep] = jnp.broadcast_to(jnp.pad(bias_ref[...], ((0, 0), (0, TILE - bias_ref.shape[1]))), (8, TILE))
     pre_sends = []
     for k in range(1, n_rep):
         pre_sends.append(send(weights.at[rep], weights.at[rep], ss_pre.at[0, k - 1], rs_pre.at[0, k - 1], rep_at(k)))
@@ -122,6 +133,8 @@
     for c in pre_sends:
         c.start()
 
+    load_cols.wait()
+    load_counts.wait()
     cols = cols_ref[...]
     shape = cols.shape
     slot = lax.broadcasted_iota(jnp.int32, shape, 1)
@@ -163,13 +176,16 @@
     agg_sends = []
     for k in order:
         tile_loads[k].wait()
-        for q in range(per):
-            p = k * per + q
-            i = block_at(p)
+
+        @pl.loop(0, per)
+        def _(q, k=k):
+            p = back_order.index(k) * per + q
+            i = ((rep + k) % n_rep) * per + q
             total = jnp.zeros((feats.shape[1], TILE), F32)
             for s in range(n_slot):
                 total += dot(feats[table_s[0, p * n_slot + s]], tiles[i, s], NT)
-            agg_mine[k, :, q * TILE:(q + 1) * TILE] = total.astype(BF16)
+            agg_mine[k, q] = total.astype(BF16)
+
         if k:
             c = send(agg_mine.at[k], agg.at[rep], ss_agg.at[k - 1], rs_agg.at[k - 1], rep_at(k))
             c.start()
@@ -178,7 +194,8 @@
     for c in agg_sends:
         c.wait_recv()
 
-    whole = agg[...].reshape(n_rep * agg.shape[1], span)
+    width = agg.shape[2]
+    whole = jnp.concatenate([agg[:, q].reshape(n_rep * width, TILE) for q in range(per)], axis=1)
     hid_sends = []
     for j in range(n_rep):
         wide_bias = jnp.concatenate([bias_col[j]] * (span // TILE), axis=1)
@@ -188,41 +205,48 @@
         delta[j] = (cots[j].astype(F32) * sigma * (1.0 + pre * (1.0 - sigma))).astype(BF16)
     deltas = delta[...].reshape(n_rep * n_hid, span)
     back_full = dot(weight_fh[...], deltas, NN).astype(BF16)
-    back_mine[...] = back_full.reshape(back_mine.shape)
+    for q in range(per):
+        back_mine[:, q] = back_full[:, q * TILE:(q + 1) * TILE].reshape(n_rep, width, TILE)
     back_sends = []
     for k in range(1, n_rep):
         c = send(back_mine.at[(rep + k) % n_rep], back.at[rep], ss_back.at[k - 1], rs_back.at[k - 1], rep_at(k))
         c.start()
         back_sends.append(c)
     back[rep] = back_mine[rep]
+    ones = jnp.ones((8, span), BF16)
+    team_sends = []
+    for j in range(n_rep):
+        grad = dot(delta[j], whole, NT)
+        bias_grad = jnp.pad(dot(ones, delta[j], NT), ((0, 0), (0, TILE - n_hid)))
+        for m in range(plane):
+            team_mine[j, m, 0:8, :] = grad[8 * m:8 * (m + 1), :]
+            team_mine[j, m, 8:16, :] = bias_grad
+    for n, (k, m) in enumerate(team):
+        c = send(
+            team_mine.at[(rep + k) % n_rep, (spot + m) % plane], team_in.at[rep, spot],
+            ss_team.at[n], rs_team.at[n], team_at(k, m),
+        )
+        c.start()
+        team_sends.append(c)
+    team_in[rep, spot] = team_mine[rep, spot]
     for k in range(1, n_rep):
         c = send(hid_mine.at[(rep + k) % n_rep], hid_out.at[:, mine], ss_hid.at[k - 1], rs_hid.at[k - 1], rep_at(k))
         c.start()
         hid_sends.append(c)
     keep_hid = pltpu.make_async_copy(hid_mine.at[rep], hid_out.at[:, mine], sem_local.at[3])
     keep_hid.start()
-    ones = jnp.ones((8, span), BF16)
-    for j in range(n_rep):
-        s1_mine[j, 0:n_hid, :] = dot(delta[j], whole, NT)
-        s1_mine[j, n_hid:n_hid + 8, :] = jnp.pad(dot(ones, delta[j], NT), ((0, 0), (0, TILE - n_hid)))
-    s1_sends = []
-    for k in range(1, n_rep):
-        c = send(s1_mine.at[(rep + k) % n_rep], s1_in.at[k - 1], ss_s1.at[k - 1], rs_s1.at[k - 1], rep_at(k))
-        c.start()
-        s1_sends.append(c)
-
-    for c in back_sends:
-        c.wait_recv()
-
-    for k in range(n_rep):
-        chunk = (rep + k) % n_rep
-        for q in range(per):
-            p = k * per + q
-            i = block_at(p)
-            lhs = back[chunk, :, q * TILE:(q + 1) * TILE]
+
+    for n, k in enumerate(back_order):
+        if k:
+            back_sends[n_rep - k - 1].wait_recv()
+
+        @pl.loop(0, per)
+        def _(q, n=n, k=k):
+            chunk = (rep + k) % n_rep
+            lhs = back[chunk, q]
             for s in range(n_slot):
-                t = p * n_slot + s
-                run[t] = dot(lhs, tiles[i, s], NN) + run[table_s[1, t]]
+                t = (n * per + q) * n_slot + s
+                run[t] = dot(lhs, tiles[chunk * per + q, s], NN) + run[table_s[1, t]]
 
     part_sends = {}
     for g in far_first:
@@ -232,59 +256,62 @@
         c.start()
         part_sends[g] = c
 
-    for c in s1_sends:
+    for c in team_sends:
         c.wait_recv()
-    mid = s1_mine[rep]
-    for k in range(1, n_rep):
-        mid += s1_in[k - 1]
-    for m in range(plane):
-        s2_mine[m, 0:8, :] = mid[8 * m:8 * (m + 1), :]
-        s2_mine[m, 8:16, :] = mid[n_hid:n_hid + 8, :]
-    s2_sends = []
-    for k in range(1, plane):
-        c = send(s2_mine.at[(spot + k) % plane], s2_in.at[spot], ss_s2.at[k - 1], rs_s2.at[k - 1], spot_at(k))
-        c.start()
-        s2_sends.append(c)
-    s2_in[spot] = s2_mine[spot]
-    for c in s2_sends:
-        c.wait_recv()
-    s3_mine[...] = sum(s2_in[m] for m in range(plane))
+    s3_mine[...] = sum(team_in[k, m] for k in range(n_rep) for m in range(plane))
     s3_sends = []
     for k in range(1, depth):
         c = send(s3_mine, s3_in.at[layer], ss_s3.at[k - 1], rs_s3.at[k - 1], layer_at(k))
         c.start()
         s3_sends.append(c)
     s3_in[layer] = s3_mine[...]
-    for c in s3_sends:
-        c.wait_recv()
-    done = sum(s3_in[m] for m in range(depth))
-    gw_mine[...] = done[0:8, :]
-    gb_out[...] = done[8:16, :]
-    my_rows = pl.ds(pl.multiple_of(spot * 8, 8), 8)
-    s4_sends = []
-    for k in range(1, plane):
-        c = send(gw_mine, gw_out.at[my_rows, :], ss_s4.at[k - 1], rs_s4.at[k - 1], spot_at(k))
-        c.start()
-        s4_sends.append(c)
-    keep_gw = pltpu.make_async_copy(gw_mine, gw_out.at[my_rows, :], sem_local.at[4])
-    keep_gw.start()
-
     for g in far_first:
         part_sends[g].wait_recv()
     for b in range(n_blk):
         value = run[table_s[2, OWN * n_blk + b]]
         for g in far_first:
             value += part_in[g, b].astype(F32)
-        gf_out[:, b * TILE:(b + 1) * TILE] = value.astype(BF16)
+        gf_mine[:, b * TILE:(b + 1) * TILE] = value.astype(BF16)
+    keep_gf = pltpu.make_async_copy(gf_mine, gf_out, sem_local.at[2])
+    keep_gf.start()
+
+    for c in s3_sends:
+        c.wait_recv()
+    done = sum(s3_in[m] for m in range(depth))
+    gw_mine[...] = done[0:8, :]
+    gb_mine[...] = done[8:16, :]
+    keep_gb = pltpu.make_async_copy(gb_mine, gb_out, sem_local.at[5])
+    keep_gb.start()
+    my_rows = pl.ds(pl.multiple_of(spot * 8, 8), 8)
+    s4_sends = []
+    for k in range(1, plane):
+        c = send(gw_mine, gw_out.at[my_rows, :], ss_s4.at[k - 1], rs_s4.at[k - 1], spot_at(k))
+        c.start()
+        s4_sends.append(c)
+    keep_gw = pltpu.make_async_copy(gw_mine, gw_out.at[my_rows, :], sem_local.at[4])
+    keep_gw.start()
 
     for c in hid_sends + s4_sends:
         c.wait_recv()
     keep_hid.wait()
     keep_gw.wait()
+    keep_gb.wait()
+    keep_gf.wait()
     everything = [feat_sends[g] for g in far_first] + pre_sends + agg_sends + back_sends + hid_sends
-    everything += s1_sends + s2_sends + s3_sends + s4_sends + [part_sends[g] for g in far_first]
+    everything += team_sends + s3_sends + s4_sends + [part_sends[g] for g in far_first]
     for c in everything:
         c.wait_send()
+
+
+def finish(hid_in, gw_in, gb_in, gf_in, hid_out, gw_out, gb_out, gf_out, gb, sems):
+    pairs = ((hid_in, hid_out), (gf_in, gf_out), (gw_in, gw_out), (gb_in, gb))
+    copies = [pltpu.make_async_copy(a, b, sems.at[n]) for n, (a, b) in enumerate(pairs)]
+    for c in copies:
+        c.start()
+    copies[3].wait()
+    gb_out[...] = gb[0:1, 0:gb_out.shape[1]]
+    for c in copies[:3]:
+        c.wait()
 
 
 def body(n_row, n_rep, plane, features, tiles, tile_cols, counts, weight, bias, cotangent):
@@ -299,7 +326,7 @@
     dma = pltpu.SemaphoreType.DMA
     vmem = pl.BlockSpec(memory_space=pltpu.VMEM)
     smem = pl.BlockSpec(memory_space=pltpu.SMEM)
-    hbm = pl.BlockSpec(memory_space=pl.ANY)
+    hbm = pl.BlockSpec(memory_space=pltpu.HBM)
 
     def pair(*shape):
         return [dma(shape), dma(shape)]
@@ -312,9 +339,12 @@
             jax.ShapeDtypeStruct((8, TILE), F32),
             jax.ShapeDtypeStruct((width, rows), BF16),
         ),
-        in_specs=[vmem, smem, vmem, hbm, hbm, hbm, hbm],
-        out_specs=(vmem, vmem, vmem, vmem),
+        in_specs=[hbm] * 7,
+        out_specs=(hbm, hbm, hbm, hbm),
         scratch_shapes=[
+            pltpu.VMEM(tile_cols.shape, jnp.int32),
+            pltpu.SMEM(counts.shape, jnp.int32),
+            pltpu.VMEM((1, n_hid), F32),
             pltpu.VMEM(tiles.shape, BF16),
             pltpu.VMEM((len(OFFSETS) * n_blk + 1, width, TILE), BF16),
             pltpu.VMEM((n_rep, n_hid, span), BF16),
@@ -325,38 +355,37 @@
             pltpu.VMEM((n_blk, TILE), jnp.int32),
             pltpu.VMEM((8, TILE), jnp.int32),
             pltpu.SMEM((8, TILE), jnp.int32),
-            pltpu.VMEM((n_rep, width, span), BF16),
-            pltpu.VMEM((n_rep, width, span), BF16),
+            pltpu.VMEM((n_rep, n_blk // n_rep, width, TILE), BF16),
+            pltpu.VMEM((n_rep, n_blk // n_rep, width, TILE), BF16),
             pltpu.VMEM((n_rep, n_hid, span), BF16),
             pltpu.VMEM((n_rep, n_hid, span), BF16),
-            pltpu.VMEM((n_rep, width, span), BF16),
-            pltpu.VMEM((n_rep, width, span), BF16),
+            pltpu.VMEM((n_rep, n_blk // n_rep, width, TILE), BF16),
+            pltpu.VMEM((n_rep, n_blk // n_rep, width, TILE), BF16),
             pltpu.VMEM((n_slots + 1, width, TILE), F32),
             pltpu.VMEM((n_far, n_blk, width, TILE), BF16),
             pltpu.VMEM((n_far, n_blk, width, TILE), BF16),
-            pltpu.VMEM((n_rep, n_hid + 8, TILE), F32),
-            pltpu.VMEM((n_rep - 1, n_hid + 8, TILE), F32),
-            pltpu.VMEM((plane, 16, TILE), F32),
-            pltpu.VMEM((plane, 16, TILE), F32),
+            pltpu.VMEM((n_rep, plane, 16, TILE), F32),
+            pltpu.VMEM((n_rep, plane, 16, TILE), F32),
             pltpu.VMEM((16, TILE), F32),
             pltpu.VMEM((depth, 16, TILE), F32),
             pltpu.VMEM((8, TILE), F32),
+            pltpu.VMEM((8, TILE), F32),
+            pltpu.VMEM((width, rows), BF16),
             dma((n_blk,)),
             dma((n_rep,)),
-            dma((5,)),
+            dma((8,)),
             *pair(n_far),
             *pair(3, n_rep - 1),
             *pair(n_rep - 1),
             *pair(n_rep - 1),
             *pair(n_rep - 1),
-            *pair(n_rep - 1),
-            *pair(plane - 1),
+            *pair(n_rep * plane - 1),
             *pair(depth - 1),
             *pair(plane - 1),
             *pair(n_far),
         ],
         compiler_params=pltpu.CompilerParams(
-            collective_id=0, has_side_effects=True, vmem_limit_bytes=32 * 1024 * 1024
+            collective_id=0, has_side_effects=True, vmem_limit_bytes=62 * 1024 * 1024
         ),
         cost_estimate=pl.CostEstimate(
             flops=4 * n_slots * TILE * TILE * width, bytes_accessed=tiles.size * 2, transcendentals=span * n_rep * n_hid
@@ -364,8 +393,20 @@
     )(
         tile_cols, counts, bias.reshape(1, n_hid), features.T, tiles, weight.T, cotangent.T,
     )
-    hidden, grad_weight, grad_bias, grad_features = out
-    return hidden.T, grad_weight.T, grad_bias[0, :n_hid], grad_features.T
+    hidden, grad_weight, grad_bias, grad_features = pl.pallas_call(
+        finish,
+        out_shape=(
+            jax.ShapeDtypeStruct((n_hid, rows), BF16),
+            jax.ShapeDtypeStruct((n_hid, fin), F32),
+            jax.ShapeDtypeStruct((1, n_hid), F32),
+            jax.ShapeDtypeStruct((width, rows), BF16),
+        ),
+        in_specs=[hbm] * 4,
+        out_specs=(hbm, hbm, vmem, hbm),
+        scratch_shapes=[pltpu.VMEM((8, TILE), F32), dma((4,))],
+        compiler_params=pltpu.CompilerParams(vmem_limit_bytes=62 * 1024 * 1024),
+    )(*out)
+    return hidden.T, grad_weight.T, grad_bias.reshape(n_hid), grad_features.T
 
 
 def solution(mesh):

time: 54.7 us -> 54 us (0.987)
  local copies, waits for them, and re-layouts: 9.05 us -> 0 us
  Pallas kernels: 44.7 us -> 53.2 us
    pallas_call x0 -> x1, Pallas kernels: none -> 8.6 us  [body(): pl.pallas_call(finish, out_shape=(jax.ShapeDtypeStruct((n_hid, rows), BF1...]
    unnamed x17 -> x0, local copies, waits for them, and re-layouts: 8.53 us -> none
where the time goes in v2:
time: 54 us; the launch traced here: 53.8 us
  Pallas kernels  53.2 us (99%)
  between operations  0.64 us (1%)
    pallas_call x1, Pallas kernels, body(): pl.pallas_call(functools.partial(kernel, n_row, n_rep, plane), out_shape=...  44.6 us
    pallas_call x1, Pallas kernels, body(): pl.pallas_call(finish, out_shape=(jax.ShapeDtypeStruct((n_hid, rows), BF1...  8.6 us

profile of v2, /device:TPU:1, one launch (start us, length us, event | category | flops | bytes accessed | tf_op | source)
XLA Modules:
  0.0 53.8 jit_solution(10106129880484797053)
XLA Ops:
  0.6 44.6 %shard_map.102 = (bf16[64,1024]{1,0:T(8,128)(2,1)}, f32[64,128]{1,0:T(8,128)}, f32[8,128]{1,0:T(8,128)}, bf16[32,1024]{1,0:T(8,128)(2,1)}) custom-call(s32[8,16]{1,0:T(8,128)} %cols_hbm.1, s32[8]{0:T(128)} %counts_hbm.1, f32[1,64]{1,0:T(1,128)} %bitcast.11, bf16[32,1024]{1,0:T(8,128)(2,1)} %bitcast.9, bf16[8,16,128,128]{3,2,1,0:T(8,128)(2,1)} %tiles_ref.1, ...), custom_call_target="tpu_custom_call" | custom-call | flops 268435456 | bytes 4194304 | tf_op jit(solution)/shard_map/pallas_call | solution.py:334
  45.2 8.6 %shard_map.103 = (bf16[64,1024]{1,0:T(8,128)(2,1)}, f32[64,128]{1,0:T(8,128)}, f32[1,64]{1,0:T(1,128)}, bf16[32,1024]{1,0:T(8,128)(2,1)}) custom-call(bf16[64,1024]{1,0:T(8,128)(2,1)} %get-tuple-element.12.hid_in, f32[64,128]{1,0:T(8,128)} %get-tuple-element.13.gw_in, f32[8,128]{1,0:T(8,128)} %get-tuple-element.14.gb_in, ...), custom_call_target="tpu_custom_call" | custom-call | tf_op jit(solution)/shard_map/pallas_call | solution.py:396

commit v3 on v2

--- a/solution.py
+++ b/solution.py
@@ -12,12 +12,19 @@
 TILE = 128
 OFFSETS = (-2, -1, 0, 1, 2, None)
 OWN = 2
+FAR = 5
+GROUP = 2
+BACK_GROUP = 2
 NT = (((1,), (1,)), ((), ()))
 NN = (((1,), (0,)), ((), ()))
 
 
 def dot(a, b, dims):
     return lax.dot_general(a, b, dims, preferred_element_type=F32)
+
+
+def join(parts):
+    return jnp.concatenate(parts, axis=1) if len(parts) > 1 else parts[0]
 
 
 def kernel(
@@ -48,6 +55,9 @@
     near_last = sorted(range(1, n_rep), key=lambda k: -hops[k])
     order = near_last + [0]
     team = [(k, m) for k in range(n_rep) for m in range(plane) if (k, m) != (0, 0)]
+    team.sort(key=lambda o: -hops[o[0]] - min(o[1], plane - o[1]) / 2)
+    spots = sorted(range(1, plane), key=lambda m: -min(m, plane - m))
+    layers = sorted(range(1, depth), key=lambda m: -min(m, depth - m))
     back_order = [0] + near_last[::-1]
 
     def block_at(p, q=0):
@@ -77,7 +87,7 @@
     barrier = pltpu.get_barrier_semaphore()
     peers = [row_at(offsets[g]) for g in far_first]
     peers += [team_at(*o) for o in team]
-    peers += [layer_at(k) for k in range(1, depth)]
+    peers += [layer_at(k) for k in layers]
     for where in peers:
         pl.semaphore_signal(barrier, inc=1, device_id=where, device_id_type=pl.DeviceIdType.MESH)
 
@@ -182,8 +192,9 @@
             p = back_order.index(k) * per + q
             i = ((rep + k) % n_rep) * per + q
             total = jnp.zeros((feats.shape[1], TILE), F32)
-            for s in range(n_slot):
-                total += dot(feats[table_s[0, p * n_slot + s]], tiles[i, s], NT)
+            for s in range(0, n_slot, GROUP):
+                some = [feats[table_s[0, p * n_slot + s + t]] for t in range(GROUP)]
+                total += dot(join(some), join([tiles[i, s + t] for t in range(GROUP)]), NT)
             agg_mine[k, q] = total.astype(BF16)
 
         if k:
@@ -217,18 +228,18 @@
     team_sends = []
     for j in range(n_rep):
         grad = dot(delta[j], whole, NT)
-        bias_grad = jnp.pad(dot(ones, delta[j], NT), ((0, 0), (0, TILE - n_hid)))
+        bias_grad = jnp.pad(dot(ones, delta[j], NT)[0:1, :], ((0, 0), (0, TILE - n_hid)))
         for m in range(plane):
             team_mine[j, m, 0:8, :] = grad[8 * m:8 * (m + 1), :]
-            team_mine[j, m, 8:16, :] = bias_grad
+            team_mine[j, m, 8:9, :] = bias_grad
     for n, (k, m) in enumerate(team):
         c = send(
-            team_mine.at[(rep + k) % n_rep, (spot + m) % plane], team_in.at[rep, spot],
+            team_mine.at[(rep + k) % n_rep, (spot + m) % plane, 0:9], team_in.at[rep, spot, 0:9],
             ss_team.at[n], rs_team.at[n], team_at(k, m),
         )
         c.start()
         team_sends.append(c)
-    team_in[rep, spot] = team_mine[rep, spot]
+    team_in[rep, spot, 0:9] = team_mine[rep, spot, 0:9]
     for k in range(1, n_rep):
         c = send(hid_mine.at[(rep + k) % n_rep], hid_out.at[:, mine], ss_hid.at[k - 1], rs_hid.at[k - 1], rep_at(k))
         c.start()
@@ -244,27 +255,48 @@
         def _(q, n=n, k=k):
             chunk = (rep + k) % n_rep
             lhs = back[chunk, q]
-            for s in range(n_slot):
-                t = (n * per + q) * n_slot + s
-                run[t] = dot(lhs, tiles[chunk * per + q, s], NN) + run[table_s[1, t]]
+            for s in range(0, n_slot, BACK_GROUP):
+                some = dot(lhs, join([tiles[chunk * per + q, s + t] for t in range(BACK_GROUP)]), NN)
+                for u in range(BACK_GROUP):
+                    t = (n * per + q) * n_slot + s + u
+                    run[t] = some[:, u * TILE:(u + 1) * TILE] + run[table_s[1, t]]
 
     part_sends = {}
     for g in far_first:
         for b in range(n_blk):
             part[g, b] = run[table_s[2, g * n_blk + b]].astype(BF16)
-        c = send(part.at[g], part_in.at[g], ss_part.at[g], rs_part.at[g], row_at(offsets[g]))
-        c.start()
-        part_sends[g] = c
+        part_sends[g] = send(
+            part.at[g], part_in.at[g], ss_part.at[g], rs_part.at[g], row_at(offsets[g])
+        )
+        if g != FAR:
+            part_sends[g].start()
 
     for c in team_sends:
         c.wait_recv()
-    s3_mine[...] = sum(team_in[k, m] for k in range(n_rep) for m in range(plane))
+    s3_mine[0:9, :] = sum(team_in[k, m, 0:9] for k in range(n_rep) for m in range(plane))
     s3_sends = []
-    for k in range(1, depth):
-        c = send(s3_mine, s3_in.at[layer], ss_s3.at[k - 1], rs_s3.at[k - 1], layer_at(k))
+    for k in layers:
+        c = send(s3_mine.at[0:9], s3_in.at[layer, 0:9], ss_s3.at[k - 1], rs_s3.at[k - 1], layer_at(k))
         c.start()
         s3_sends.append(c)
-    s3_in[layer] = s3_mine[...]
+    part_sends[FAR].start()
+    s3_in[layer, 0:9] = s3_mine[0:9, :]
+    for c in s3_sends:
+        c.wait_recv()
+    done = sum(s3_in[m, 0:9] for m in range(depth))
+    gw_mine[...] = done[0:8, :]
+    gb_mine[...] = jnp.broadcast_to(done[8:9, :], gb_mine.shape)
+    keep_gb = pltpu.make_async_copy(gb_mine, gb_out, sem_local.at[5])
+    keep_gb.start()
+    my_rows = pl.ds(pl.multiple_of(spot * 8, 8), 8)
+    s4_sends = []
+    for k in spots:
+        c = send(gw_mine, gw_out.at[my_rows, :], ss_s4.at[k - 1], rs_s4.at[k - 1], spot_at(k))
+        c.start()
+        s4_sends.append(c)
+    keep_gw = pltpu.make_async_copy(gw_mine, gw_out.at[my_rows, :], sem_local.at[4])
+    keep_gw.start()
+
     for g in far_first:
         part_sends[g].wait_recv()
     for b in range(n_blk):
@@ -274,22 +306,6 @@
         gf_mine[:, b * TILE:(b + 1) * TILE] = value.astype(BF16)
     keep_gf = pltpu.make_async_copy(gf_mine, gf_out, sem_local.at[2])
     keep_gf.start()
-
-    for c in s3_sends:
-        c.wait_recv()
-    done = sum(s3_in[m] for m in range(depth))
-    gw_mine[...] = done[0:8, :]
-    gb_mine[...] = done[8:16, :]
-    keep_gb = pltpu.make_async_copy(gb_mine, gb_out, sem_local.at[5])
-    keep_gb.start()
-    my_rows = pl.ds(pl.multiple_of(spot * 8, 8), 8)
-    s4_sends = []
-    for k in range(1, plane):
-        c = send(gw_mine, gw_out.at[my_rows, :], ss_s4.at[k - 1], rs_s4.at[k - 1], spot_at(k))
-        c.start()
-        s4_sends.append(c)
-    keep_gw = pltpu.make_async_copy(gw_mine, gw_out.at[my_rows, :], sem_local.at[4])
-    keep_gw.start()
 
     for c in hid_sends + s4_sends:
         c.wait_recv()
@@ -303,14 +319,19 @@
         c.wait_send()
 
 
-def finish(hid_in, gw_in, gb_in, gf_in, hid_out, gw_out, gb_out, gf_out, gb, sems):
-    pairs = ((hid_in, hid_out), (gf_in, gf_out), (gw_in, gw_out), (gb_in, gb))
-    copies = [pltpu.make_async_copy(a, b, sems.at[n]) for n, (a, b) in enumerate(pairs)]
-    for c in copies:
-        c.start()
-    copies[3].wait()
+def finish(hid_in, gw_in, gb_in, gf_in, hid_out, gw_out, gb_out, gf_out, hid, gw, gb, gf, sems):
+    through = ((hid_in, hid, hid_out), (gf_in, gf, gf_out), (gw_in, gw, gw_out))
+    loads = [pltpu.make_async_copy(a, b, sems.at[0, n]) for n, (a, b, c) in enumerate(through)]
+    loads.append(pltpu.make_async_copy(gb_in, gb, sems.at[0, 3]))
+    stores = [pltpu.make_async_copy(b, c, sems.at[1, n]) for n, (a, b, c) in enumerate(through)]
+    for c in loads:
+        c.start()
+    for n, c in enumerate(stores):
+        loads[n].wait()
+        c.start()
+    loads[3].wait()
     gb_out[...] = gb[0:1, 0:gb_out.shape[1]]
-    for c in copies[:3]:
+    for c in stores:
         c.wait()
 
 
@@ -403,7 +424,13 @@
         ),
         in_specs=[hbm] * 4,
         out_specs=(hbm, hbm, vmem, hbm),
-        scratch_shapes=[pltpu.VMEM((8, TILE), F32), dma((4,))],
+        scratch_shapes=[
+            pltpu.VMEM((n_hid, rows), BF16),
+            pltpu.VMEM((n_hid, fin), F32),
+            pltpu.VMEM((8, TILE), F32),
+            pltpu.VMEM((width, rows), BF16),
+            dma((2, 4)),
+        ],
         compiler_params=pltpu.CompilerParams(vmem_limit_bytes=62 * 1024 * 1024),
     )(*out)
     return hidden.T, grad_weight.T, grad_bias.reshape(n_hid), grad_features.T

time: 54 us -> 42.9 us (0.79)
  Pallas kernels: 53.2 us -> 42.2 us
    pallas_call x1, Pallas kernels: 8.6 us -> 2.16 us  [body(): pl.pallas_call(finish, out_shape=(jax.ShapeDtypeStruct((n_hid, rows), BF1...]
    pallas_call x1, Pallas kernels: 44.6 us -> 40 us  [body(): pl.pallas_call(functools.partial(kernel, n_row, n_rep, plane), out_shape=...]
where the time goes in v3:
time: 42.9 us
  Pallas kernels  42.2 us (98%)
  between operations  0.64 us (1%)
    pallas_call x1, Pallas kernels, body(): pl.pallas_call(functools.partial(kernel, n_row, n_rep, plane), out_shape=...  40 us
    pallas_call x1, Pallas kernels, body(): pl.pallas_call(finish, out_shape=(jax.ShapeDtypeStruct((n_hid, rows), BF1...  2.16 us

profile of v3, /device:TPU:1, one launch (start us, length us, event | category | flops | bytes accessed | tf_op | source)
XLA Modules:
  0.0 42.9 jit_solution(12784898862128552913)
XLA Ops:
  0.6 40.0 %shard_map.102 = (bf16[64,1024]{1,0:T(8,128)(2,1)}, f32[64,128]{1,0:T(8,128)}, f32[8,128]{1,0:T(8,128)}, bf16[32,1024]{1,0:T(8,128)(2,1)}) custom-call(s32[8,16]{1,0:T(8,128)} %cols_hbm.1, s32[8]{0:T(128)} %counts_hbm.1, f32[1,64]{1,0:T(1,128)} %bitcast.11, bf16[32,1024]{1,0:T(8,128)(2,1)} %bitcast.9, bf16[8,16,128,128]{3,2,1,0:T(8,128)(2,1)} %tiles_ref.1, ...), custom_call_target="tpu_custom_call" | custom-call | flops 268435456 | bytes 4194304 | tf_op jit(solution)/shard_map/pallas_call | solution.py:355
  40.7 2.2 %shard_map.103 = (bf16[64,1024]{1,0:T(8,128)(2,1)}, f32[64,128]{1,0:T(8,128)}, f32[1,64]{1,0:T(1,128)}, bf16[32,1024]{1,0:T(8,128)(2,1)}) custom-call(bf16[64,1024]{1,0:T(8,128)(2,1)} %get-tuple-element.12.hid_in, f32[64,128]{1,0:T(8,128)} %get-tuple-element.13.gw_in, f32[8,128]{1,0:T(8,128)} %get-tuple-element.14.gb_in, ...), custom_call_target="tpu_custom_call" | custom-call | tf_op jit(solution)/shard_map/pallas_call | solution.py:417

commit v4 on v3

--- a/solution.py
+++ b/solution.py
@@ -51,6 +51,7 @@
     n_slots = n_blk * n_slot
     offsets = [n_row // 2 if o is None else o for o in OFFSETS]
     far_first = (5, 0, 4, 1, 3)
+    feat_order = (0, 5, 4, 1, 3)
     hops = [min(k, n_rep - k) for k in range(n_rep)]
     near_last = sorted(range(1, n_rep), key=lambda k: -hops[k])
     order = near_last + [0]
@@ -125,7 +126,7 @@
         )
         for g in far_first
     }
-    for g in far_first:
+    for g in feat_order:
         feat_sends[g].start()
     load_w.wait()
     load_bias.wait()
@@ -172,14 +173,6 @@
     run[n_slots] = jnp.zeros(run.shape[1:], F32)
     to_scalar.wait()
 
-    for c in pre_sends:
-        c.wait_recv()
-    load_c.wait()
-    n_hid = weights.shape[1]
-    for j in range(n_rep):
-        weight_fh[:, j * n_hid:(j + 1) * n_hid] = weights[j].astype(F32).T.astype(BF16)
-        bias_col[j] = jnp.broadcast_to(biases[j, 0:1, :], (TILE, TILE)).T[0:n_hid, :]
-
     for g in far_first:
         feat_sends[g].wait_recv()
 
@@ -202,6 +195,15 @@
             c.start()
             agg_sends.append(c)
     agg[rep] = agg_mine[0]
+
+    for c in pre_sends:
+        c.wait_recv()
+    load_c.wait()
+    n_hid = weights.shape[1]
+    for j in range(n_rep):
+        weight_fh[:, j * n_hid:(j + 1) * n_hid] = weights[j].astype(F32).T.astype(BF16)
+        bias_col[j] = jnp.broadcast_to(biases[j, 0:1, :], (TILE, TILE)).T[0:n_hid, :]
+
     for c in agg_sends:
         c.wait_recv()
 
@@ -218,12 +220,6 @@
     back_full = dot(weight_fh[...], deltas, NN).astype(BF16)
     for q in range(per):
         back_mine[:, q] = back_full[:, q * TILE:(q + 1) * TILE].reshape(n_rep, width, TILE)
-    back_sends = []
-    for k in range(1, n_rep):
-        c = send(back_mine.at[(rep + k) % n_rep], back.at[rep], ss_back.at[k - 1], rs_back.at[k - 1], rep_at(k))
-        c.start()
-        back_sends.append(c)
-    back[rep] = back_mine[rep]
     ones = jnp.ones((8, span), BF16)
     team_sends = []
     for j in range(n_rep):
@@ -232,6 +228,12 @@
         for m in range(plane):
             team_mine[j, m, 0:8, :] = grad[8 * m:8 * (m + 1), :]
             team_mine[j, m, 8:9, :] = bias_grad
+    back_sends = []
+    for k in range(1, n_rep):
+        c = send(back_mine.at[(rep + k) % n_rep], back.at[rep], ss_back.at[k - 1], rs_back.at[k - 1], rep_at(k))
+        c.start()
+        back_sends.append(c)
+    back[rep] = back_mine[rep]
     for n, (k, m) in enumerate(team):
         c = send(
             team_mine.at[(rep + k) % n_rep, (spot + m) % plane, 0:9], team_in.at[rep, spot, 0:9],
@@ -240,13 +242,6 @@
         c.start()
         team_sends.append(c)
     team_in[rep, spot, 0:9] = team_mine[rep, spot, 0:9]
-    for k in range(1, n_rep):
-        c = send(hid_mine.at[(rep + k) % n_rep], hid_out.at[:, mine], ss_hid.at[k - 1], rs_hid.at[k - 1], rep_at(k))
-        c.start()
-        hid_sends.append(c)
-    keep_hid = pltpu.make_async_copy(hid_mine.at[rep], hid_out.at[:, mine], sem_local.at[3])
-    keep_hid.start()
-
     for n, k in enumerate(back_order):
         if k:
             back_sends[n_rep - k - 1].wait_recv()
@@ -261,6 +256,14 @@
                     t = (n * per + q) * n_slot + s + u
                     run[t] = some[:, u * TILE:(u + 1) * TILE] + run[table_s[1, t]]
 
+    for c in team_sends:
+        c.wait_recv()
+    s3_mine[0:9, :] = sum(team_in[k, m, 0:9] for k in range(n_rep) for m in range(plane))
+    s3_sends = []
+    for k in layers:
+        c = send(s3_mine.at[0:9], s3_in.at[layer, 0:9], ss_s3.at[k - 1], rs_s3.at[k - 1], layer_at(k))
+        c.start()
+        s3_sends.append(c)
     part_sends = {}
     for g in far_first:
         for b in range(n_blk):
@@ -268,19 +271,16 @@
         part_sends[g] = send(
             part.at[g], part_in.at[g], ss_part.at[g], rs_part.at[g], row_at(offsets[g])
         )
-        if g != FAR:
-            part_sends[g].start()
-
-    for c in team_sends:
-        c.wait_recv()
-    s3_mine[0:9, :] = sum(team_in[k, m, 0:9] for k in range(n_rep) for m in range(plane))
-    s3_sends = []
-    for k in layers:
-        c = send(s3_mine.at[0:9], s3_in.at[layer, 0:9], ss_s3.at[k - 1], rs_s3.at[k - 1], layer_at(k))
-        c.start()
-        s3_sends.append(c)
-    part_sends[FAR].start()
+        part_sends[g].start()
+
     s3_in[layer, 0:9] = s3_mine[0:9, :]
+    for k in range(1, n_rep):
+        c = send(hid_mine.at[(rep + k) % n_rep], hid_out.at[:, mine], ss_hid.at[k - 1], rs_hid.at[k - 1], rep_at(k))
+        c.start()
+        hid_sends.append(c)
+    keep_hid = pltpu.make_async_copy(hid_mine.at[rep], hid_out.at[:, mine], sem_local.at[3])
+    keep_hid.start()
+
     for c in s3_sends:
         c.wait_recv()
     done = sum(s3_in[m, 0:9] for m in range(depth))

time: 42.9 us -> 42.1 us (0.981)
  Pallas kernels: 42.2 us -> 41.3 us
    pallas_call x1, Pallas kernels: 40 us -> 39.2 us  [body(): pl.pallas_call(functools.partial(kernel, n_row, n_rep, plane), out_shape=...]
where the time goes in v4:
time: 42.1 us; the launch traced here: 42 us
  Pallas kernels  41.3 us (98%)
  between operations  0.64 us (2%)
    pallas_call x1, Pallas kernels, body(): pl.pallas_call(functools.partial(kernel, n_row, n_rep, plane), out_shape=...  39.2 us
    pallas_call x1, Pallas kernels, body(): pl.pallas_call(finish, out_shape=(jax.ShapeDtypeStruct((n_hid, rows), BF1...  2.16 us

profile of v4, /device:TPU:1, one launch (start us, length us, event | category | flops | bytes accessed | tf_op | source)
XLA Modules:
  0.0 42.0 jit_solution(885304011531713277)
XLA Ops:
  0.6 39.2 %shard_map.102 = (bf16[64,1024]{1,0:T(8,128)(2,1)}, f32[64,128]{1,0:T(8,128)}, f32[8,128]{1,0:T(8,128)}, bf16[32,1024]{1,0:T(8,128)(2,1)}) custom-call(s32[8,16]{1,0:T(8,128)} %cols_hbm.1, s32[8]{0:T(128)} %counts_hbm.1, f32[1,64]{1,0:T(1,128)} %bitcast.11, bf16[32,1024]{1,0:T(8,128)(2,1)} %bitcast.9, bf16[8,16,128,128]{3,2,1,0:T(8,128)(2,1)} %tiles_ref.1, ...), custom_call_target="tpu_custom_call" | custom-call | flops 268435456 | bytes 4194304 | tf_op jit(solution)/shard_map/pallas_call | solution.py:355
  39.8 2.2 %shard_map.103 = (bf16[64,1024]{1,0:T(8,128)(2,1)}, f32[64,128]{1,0:T(8,128)}, f32[1,64]{1,0:T(1,128)}, bf16[32,1024]{1,0:T(8,128)(2,1)}) custom-call(bf16[64,1024]{1,0:T(8,128)(2,1)} %get-tuple-element.12.hid_in, f32[64,128]{1,0:T(8,128)} %get-tuple-element.13.gw_in, f32[8,128]{1,0:T(8,128)} %get-tuple-element.14.gb_in, ...), custom_call_target="tpu_custom_call" | custom-call | tf_op jit(solution)/shard_map/pallas_call | solution.py:417

commit v5 on v4

--- a/solution.py
+++ b/solution.py
@@ -51,14 +51,18 @@
     n_slots = n_blk * n_slot
     offsets = [n_row // 2 if o is None else o for o in OFFSETS]
     far_first = (5, 0, 4, 1, 3)
-    feat_order = (0, 5, 4, 1, 3)
+    feat_order = (0, 4, 5, 1, 3)
     hops = [min(k, n_rep - k) for k in range(n_rep)]
     near_last = sorted(range(1, n_rep), key=lambda k: -hops[k])
     order = near_last + [0]
-    team = [(k, m) for k in range(n_rep) for m in range(plane) if (k, m) != (0, 0)]
-    team.sort(key=lambda o: -hops[o[0]] - min(o[1], plane - o[1]) / 2)
-    spots = sorted(range(1, plane), key=lambda m: -min(m, plane - m))
-    layers = sorted(range(1, depth), key=lambda m: -min(m, depth - m))
+    n_x = plane // 2
+    chip = spot // 2
+    core = spot % 2
+    team = [(k, m) for k in range(n_rep) for m in range(n_x) if (k, m) != (0, 0)]
+    team.sort(key=lambda o: -hops[o[0]] - min(o[1], n_x - o[1]))
+    column = [(k, c) for k in range(depth) for c in range(2) if (k, c) != (0, 0)]
+    column.sort(key=lambda o: -min(o[0], depth - o[0]))
+    chips = sorted(range(1, n_x), key=lambda m: -min(m, n_x - m))
     back_order = [0] + near_last[::-1]
 
     def block_at(p, q=0):
@@ -71,13 +75,10 @@
         return {"row": row, "rep": (rep + k) % n_rep}
 
     def team_at(k, m):
-        return {"row": layer * plane + (spot + m) % plane, "rep": (rep + k) % n_rep}
-
-    def spot_at(k):
-        return {"row": layer * plane + (spot + k) % plane, "rep": rep}
-
-    def layer_at(k):
-        return {"row": ((layer + k) % depth) * plane + spot, "rep": rep}
+        return {"row": layer * plane + (chip + m) % n_x * 2 + core, "rep": (rep + k) % n_rep}
+
+    def column_at(k, c):
+        return {"row": (layer + k) % depth * plane + chip * 2 + (core + c) % 2, "rep": rep}
 
     def send(src, dst, ss, rs, where):
         return pltpu.make_async_remote_copy(
@@ -88,7 +89,7 @@
     barrier = pltpu.get_barrier_semaphore()
     peers = [row_at(offsets[g]) for g in far_first]
     peers += [team_at(*o) for o in team]
-    peers += [layer_at(k) for k in layers]
+    peers += [column_at(*o) for o in column]
     for where in peers:
         pl.semaphore_signal(barrier, inc=1, device_id=where, device_id_type=pl.DeviceIdType.MESH)
 
@@ -225,9 +226,9 @@
     for j in range(n_rep):
         grad = dot(delta[j], whole, NT)
         bias_grad = jnp.pad(dot(ones, delta[j], NT)[0:1, :], ((0, 0), (0, TILE - n_hid)))
-        for m in range(plane):
-            team_mine[j, m, 0:8, :] = grad[8 * m:8 * (m + 1), :]
-            team_mine[j, m, 8:9, :] = bias_grad
+        for m in range(n_x):
+            team_mine[j, m, 0:16, :] = grad[16 * m:16 * (m + 1), :]
+            team_mine[j, m, 16:17, :] = bias_grad
     back_sends = []
     for k in range(1, n_rep):
         c = send(back_mine.at[(rep + k) % n_rep], back.at[rep], ss_back.at[k - 1], rs_back.at[k - 1], rep_at(k))
@@ -236,12 +237,12 @@
     back[rep] = back_mine[rep]
     for n, (k, m) in enumerate(team):
         c = send(
-            team_mine.at[(rep + k) % n_rep, (spot + m) % plane, 0:9], team_in.at[rep, spot, 0:9],
+            team_mine.at[(rep + k) % n_rep, (chip + m) % n_x, 0:17], team_in.at[rep, chip, 0:17],
             ss_team.at[n], rs_team.at[n], team_at(k, m),
         )
         c.start()
         team_sends.append(c)
-    team_in[rep, spot, 0:9] = team_mine[rep, spot, 0:9]
+    team_in[rep, chip, 0:17] = team_mine[rep, chip, 0:17]
     for n, k in enumerate(back_order):
         if k:
             back_sends[n_rep - k - 1].wait_recv()
@@ -258,14 +259,14 @@
 
     for c in team_sends:
         c.wait_recv()
-    s3_mine[0:9, :] = sum(team_in[k, m, 0:9] for k in range(n_rep) for m in range(plane))
+    s3_mine[0:17, :] = sum(team_in[k, m, 0:17] for k in range(n_rep) for m in range(n_x))
     s3_sends = []
-    for k in layers:
-        c = send(s3_mine.at[0:9], s3_in.at[layer, 0:9], ss_s3.at[k - 1], rs_s3.at[k - 1], layer_at(k))
+    for n, o in enumerate(column):
+        c = send(s3_mine.at[0:17], s3_in.at[layer, core, 0:17], ss_s3.at[n], rs_s3.at[n], column_at(*o))
         c.start()
         s3_sends.append(c)
     part_sends = {}
-    for g in far_first:
+    for g in feat_order:
         for b in range(n_blk):
             part[g, b] = run[table_s[2, g * n_blk + b]].astype(BF16)
         part_sends[g] = send(
@@ -273,7 +274,7 @@
         )
         part_sends[g].start()
 
-    s3_in[layer, 0:9] = s3_mine[0:9, :]
+    s3_in[layer, core, 0:17] = s3_mine[0:17, :]
     for k in range(1, n_rep):
         c = send(hid_mine.at[(rep + k) % n_rep], hid_out.at[:, mine], ss_hid.at[k - 1], rs_hid.at[k - 1], rep_at(k))
         c.start()
@@ -283,15 +284,15 @@
 
     for c in s3_sends:
         c.wait_recv()
-    done = sum(s3_in[m, 0:9] for m in range(depth))
-    gw_mine[...] = done[0:8, :]
-    gb_mine[...] = jnp.broadcast_to(done[8:9, :], gb_mine.shape)
+    done = sum(s3_in[m, c, 0:17] for m in range(depth) for c in range(2))
+    gw_mine[...] = done[0:16, :]
+    gb_mine[...] = jnp.broadcast_to(done[16:17, :], gb_mine.shape)
     keep_gb = pltpu.make_async_copy(gb_mine, gb_out, sem_local.at[5])
     keep_gb.start()
-    my_rows = pl.ds(pl.multiple_of(spot * 8, 8), 8)
+    my_rows = pl.ds(pl.multiple_of(chip * 16, 16), 16)
     s4_sends = []
-    for k in spots:
-        c = send(gw_mine, gw_out.at[my_rows, :], ss_s4.at[k - 1], rs_s4.at[k - 1], spot_at(k))
+    for k in chips:
+        c = send(gw_mine, gw_out.at[my_rows, :], ss_s4.at[k - 1], rs_s4.at[k - 1], team_at(0, k))
         c.start()
         s4_sends.append(c)
     keep_gw = pltpu.make_async_copy(gw_mine, gw_out.at[my_rows, :], sem_local.at[4])
@@ -385,11 +386,11 @@
             pltpu.VMEM((n_slots + 1, width, TILE), F32),
             pltpu.VMEM((n_far, n_blk, width, TILE), BF16),
             pltpu.VMEM((n_far, n_blk, width, TILE), BF16),
-            pltpu.VMEM((n_rep, plane, 16, TILE), F32),
-            pltpu.VMEM((n_rep, plane, 16, TILE), F32),
+            pltpu.VMEM((n_rep, plane // 2, 24, TILE), F32),
+            pltpu.VMEM((n_rep, plane // 2, 24, TILE), F32),
+            pltpu.VMEM((24, TILE), F32),
+            pltpu.VMEM((depth, 2, 24, TILE), F32),
             pltpu.VMEM((16, TILE), F32),
-            pltpu.VMEM((depth, 16, TILE), F32),
-            pltpu.VMEM((8, TILE), F32),
             pltpu.VMEM((8, TILE), F32),
             pltpu.VMEM((width, rows), BF16),
             dma((n_blk,)),
@@ -400,9 +401,9 @@
             *pair(n_rep - 1),
             *pair(n_rep - 1),
             *pair(n_rep - 1),
-            *pair(n_rep * plane - 1),
-            *pair(depth - 1),
-            *pair(plane - 1),
+            *pair(n_rep * plane // 2 - 1),
+            *pair(depth * 2 - 1),
+            *pair(plane // 2 - 1),
             *pair(n_far),
         ],
         compiler_params=pltpu.CompilerParams(

time: 42.1 us -> 41.8 us (level)
  no operation moved by 1% of the time
where the time goes in v5:
time: 41.8 us; the launch traced here: 41.7 us
  Pallas kernels  41.1 us (98%)
  between operations  0.64 us (2%)
    pallas_call x1, Pallas kernels, body(): pl.pallas_call(functools.partial(kernel, n_row, n_rep, plane), out_shape=...  38.9 us
    pallas_call x1, Pallas kernels, body(): pl.pallas_call(finish, out_shape=(jax.ShapeDtypeStruct((n_hid, rows), BF1...  2.16 us

profile of v5, /device:TPU:1, one launch (start us, length us, event | category | flops | bytes accessed | tf_op | source)
XLA Modules:
  0.0 41.7 jit_solution(13063872612033742004)
XLA Ops:
  0.6 38.9 %shard_map.102 = (bf16[64,1024]{1,0:T(8,128)(2,1)}, f32[64,128]{1,0:T(8,128)}, f32[8,128]{1,0:T(8,128)}, bf16[32,1024]{1,0:T(8,128)(2,1)}) custom-call(s32[8,16]{1,0:T(8,128)} %cols_hbm.1, s32[8]{0:T(128)} %counts_hbm.1, f32[1,64]{1,0:T(1,128)} %bitcast.11, bf16[32,1024]{1,0:T(8,128)(2,1)} %bitcast.9, bf16[8,16,128,128]{3,2,1,0:T(8,128)(2,1)} %tiles_ref.1, ...), custom_call_target="tpu_custom_call" | custom-call | flops 268435456 | bytes 4194304 | tf_op jit(solution)/shard_map/pallas_call | solution.py:356
  39.6 2.2 %shard_map.103 = (bf16[64,1024]{1,0:T(8,128)(2,1)}, f32[64,128]{1,0:T(8,128)}, f32[1,64]{1,0:T(1,128)}, bf16[32,1024]{1,0:T(8,128)(2,1)}) custom-call(bf16[64,1024]{1,0:T(8,128)(2,1)} %get-tuple-element.12.hid_in, f32[64,128]{1,0:T(8,128)} %get-tuple-element.13.gw_in, f32[8,128]{1,0:T(8,128)} %get-tuple-element.14.gb_in, ...), custom_call_target="tpu_custom_call" | custom-call | tf_op jit(solution)/shard_map/pallas_call | solution.py:418

commit v6 on v5

--- a/solution.py
+++ b/solution.py
@@ -181,7 +181,7 @@
     for k in order:
         tile_loads[k].wait()
 
-        @pl.loop(0, per)
+        @pl.loop(0, per, unroll=True)
         def _(q, k=k):
             p = back_order.index(k) * per + q
             i = ((rep + k) % n_rep) * per + q
@@ -247,7 +247,7 @@
         if k:
             back_sends[n_rep - k - 1].wait_recv()
 
-        @pl.loop(0, per)
+        @pl.loop(0, per, unroll=True)
         def _(q, n=n, k=k):
             chunk = (rep + k) % n_rep
             lhs = back[chunk, q]

time: 41.8 us -> 41.3 us (0.988)
  Pallas kernels: 41.1 us -> 40.5 us
    pallas_call x1, Pallas kernels: 38.9 us -> 38.4 us  [body(): pl.pallas_call(functools.partial(kernel, n_row, n_rep, plane), out_shape=...]
where the time goes in v6:
time: 41.3 us; the launch traced here: 41.2 us
  Pallas kernels  40.5 us (98%)
  between operations  0.64 us (2%)
    pallas_call x1, Pallas kernels, body(): pl.pallas_call(functools.partial(kernel, n_row, n_rep, plane), out_shape=...  38.4 us
    pallas_call x1, Pallas kernels, body(): pl.pallas_call(finish, out_shape=(jax.ShapeDtypeStruct((n_hid, rows), BF1...  2.16 us

profile of v6, /device:TPU:1, one launch (start us, length us, event | category | flops | bytes accessed | tf_op | source)
XLA Modules:
  0.0 41.2 jit_solution(7829642893210591633)
XLA Ops:
  0.6 38.4 %shard_map.102 = (bf16[64,1024]{1,0:T(8,128)(2,1)}, f32[64,128]{1,0:T(8,128)}, f32[8,128]{1,0:T(8,128)}, bf16[32,1024]{1,0:T(8,128)(2,1)}) custom-call(s32[8,16]{1,0:T(8,128)} %cols_hbm.1, s32[8]{0:T(128)} %counts_hbm.1, f32[1,64]{1,0:T(1,128)} %bitcast.11, bf16[32,1024]{1,0:T(8,128)(2,1)} %bitcast.9, bf16[8,16,128,128]{3,2,1,0:T(8,128)(2,1)} %tiles_ref.1, ...), custom_call_target="tpu_custom_call" | custom-call | flops 268435456 | bytes 4194304 | tf_op jit(solution)/shard_map/pallas_call | solution.py:356
  39.0 2.2 %shard_map.103 = (bf16[64,1024]{1,0:T(8,128)(2,1)}, f32[64,128]{1,0:T(8,128)}, f32[1,64]{1,0:T(1,128)}, bf16[32,1024]{1,0:T(8,128)(2,1)}) custom-call(bf16[64,1024]{1,0:T(8,128)(2,1)} %get-tuple-element.12.hid_in, f32[64,128]{1,0:T(8,128)} %get-tuple-element.13.gw_in, f32[8,128]{1,0:T(8,128)} %get-tuple-element.14.gb_in, ...), custom_call_target="tpu_custom_call" | custom-call | tf_op jit(solution)/shard_map/pallas_call | solution.py:418

commit v7 on v6

--- a/solution.py
+++ b/solution.py
@@ -13,8 +13,8 @@
 OFFSETS = (-2, -1, 0, 1, 2, None)
 OWN = 2
 FAR = 5
-GROUP = 2
-BACK_GROUP = 2
+GROUP = 4
+BACK_GROUP = 4
 NT = (((1,), (1,)), ((), ()))
 NN = (((1,), (0,)), ((), ()))
 

time: 41.3 us -> 41.3 us (level)
  no operation moved by 1% of the time
where the time goes in v7:
time: 41.3 us; the launch traced here: 41.2 us
  Pallas kernels  40.6 us (98%)
  between operations  0.64 us (2%)
    pallas_call x1, Pallas kernels, body(): pl.pallas_call(functools.partial(kernel, n_row, n_rep, plane), out_shape=...  38.4 us
    pallas_call x1, Pallas kernels, body(): pl.pallas_call(finish, out_shape=(jax.ShapeDtypeStruct((n_hid, rows), BF1...  2.16 us

profile of v7, /device:TPU:1, one launch (start us, length us, event | category | flops | bytes accessed | tf_op | source)
XLA Modules:
  0.0 41.2 jit_solution(11418556760509675381)
XLA Ops:
  0.6 38.4 %shard_map.102 = (bf16[64,1024]{1,0:T(8,128)(2,1)}, f32[64,128]{1,0:T(8,128)}, f32[8,128]{1,0:T(8,128)}, bf16[32,1024]{1,0:T(8,128)(2,1)}) custom-call(s32[8,16]{1,0:T(8,128)} %cols_hbm.1, s32[8]{0:T(128)} %counts_hbm.1, f32[1,64]{1,0:T(1,128)} %bitcast.11, bf16[32,1024]{1,0:T(8,128)(2,1)} %bitcast.9, bf16[8,16,128,128]{3,2,1,0:T(8,128)(2,1)} %tiles_ref.1, ...), custom_call_target="tpu_custom_call" | custom-call | flops 268435456 | bytes 4194304 | tf_op jit(solution)/shard_map/pallas_call | solution.py:356
  39.1 2.2 %shard_map.103 = (bf16[64,1024]{1,0:T(8,128)(2,1)}, f32[64,128]{1,0:T(8,128)}, f32[1,64]{1,0:T(1,128)}, bf16[32,1024]{1,0:T(8,128)(2,1)}) custom-call(bf16[64,1024]{1,0:T(8,128)(2,1)} %get-tuple-element.12.hid_in, f32[64,128]{1,0:T(8,128)} %get-tuple-element.13.gw_in, f32[8,128]{1,0:T(8,128)} %get-tuple-element.14.gb_in, ...), custom_call_target="tpu_custom_call" | custom-call | tf_op jit(solution)/shard_map/pallas_call | solution.py:418
